TPU v7x, 32 devices: a whole 2x2x4 slice. The times are simulated.
32 devices in a mesh: grp: 2 (over x), tile: 2 (over core), cond: 8 (over z, y).
Axes of the slice: x: 2, y: 2, z: 4, core: 2. Of those that a mesh axis runs over, the one named last changes fastest.
Arguments:
- latent: float32 [4096, 128], P(('grp', 'cond'), 'tile'), parts along dimension 0, may hold values from -8 to 8
- target: int32 [4096, 128], P('grp'), parts along dimension 0, may hold values 0 or 1
- kernel_table: float32 [8, 8, 2, 65, 65], replicated, may hold values from -4.5 to 4.5
- socs_weights: float32 [8], replicated, may hold values from 0.25 to 2.5
- dose_levels: float32 [4], replicated, may hold values from 0.8 to 1.25
- cond_focus: int32 [8], replicated, may hold values from 0 to 7, each once
- cond_dose: int32 [8], replicated, may hold values from 0 to 3
Outputs:
- mask_gradient: float32 [4096, 128], P(('grp', 'cond'), 'tile'), parts along dimension 0
- worst_loss: float32 [2], P('grp'), parts along dimension 0
There are 2 independent parts, one for each index of `grp`. A program takes and returns all parts, laid end to end along the dimension named above; an argument that names none is the same for every part. Nothing has to cross between parts.
Inputs may be any that keep to these rules, and one draw needn't show every extreme that they name: `cond_focus`: each focus level is named by exactly one condition.
All inputs are finite; a program needn't handle non-finite values.
Results may differ from a plain program's by a relative error of at most 0.0003.
Values sent between devices are 32-bit elements; how exact they have to be, the bound alone decides.
A program may use at most 64 MiB of HBM per device.

v0:
```python
import math

import jax
import jax.numpy as jnp
from jax import lax
from jax.sharding import PartitionSpec as P

TILE = 128
HALO = 16
NF = 65
EXT = 160


STEEPNESS = 4.0
THRESHOLD = 1.0
SHARPNESS = 6.0
GRAD_GAIN = 256.0
PRECISE = lax.Precision.HIGHEST


def with_halo(cells, sides, width):
    for axis, dim in sides:
        count = lax.axis_size(axis)
        ends = count - 1
        head = lax.slice_in_dim(cells, 0, width, axis=dim)
        tail = lax.slice_in_dim(cells, cells.shape[dim] - width, cells.shape[dim], axis=dim)
        cells = jnp.concatenate(
            [
                lax.ppermute(tail, axis, [(i, (i + 1) % count) for i in range(ends)]),
                cells,
                lax.ppermute(head, axis, [((i + 1) % count, i) for i in range(ends)]),
            ],
            axis=dim,
        )
    return cells


def make_tables(freq_count, period, offset, extent):
    frequency = jnp.arange(freq_count, dtype=jnp.int32) - (freq_count - 1) // 2
    position = jnp.arange(extent, dtype=jnp.int32) + offset
    product = frequency[:, None] * position[None, :] % period
    phases = product.astype(jnp.float32) * (2.0 * math.pi / period)
    return (jnp.cos(phases), jnp.sin(phases))


def tile_error(tile_block, spectra, weights, dose, target_tile, tables):
    cos_full, sin_full, cos_core, sin_core = tables
    col_real = jnp.dot(tile_block, cos_core.T, precision=PRECISE)
    col_imag = -jnp.dot(tile_block, sin_core.T, precision=PRECISE)
    spec_real = jnp.dot(cos_full, col_real, precision=PRECISE) + jnp.dot(
        sin_full, col_imag, precision=PRECISE
    )
    spec_imag = jnp.dot(cos_full, col_imag, precision=PRECISE) - jnp.dot(
        sin_full, col_real, precision=PRECISE
    )
    inverse_area = 1.0 / (cos_full.shape[1] * cos_full.shape[1])
    kern_real = spectra[:, 0]
    kern_imag = spectra[:, 1]
    prod_real = (kern_real * spec_real - kern_imag * spec_imag) * inverse_area
    prod_imag = (kern_real * spec_imag + kern_imag * spec_real) * inverse_area
    half_real = jnp.einsum("kfg,gy->kfy", prod_real, cos_core, precision=PRECISE) - jnp.einsum(
        "kfg,gy->kfy", prod_imag, sin_core, precision=PRECISE
    )
    half_imag = jnp.einsum("kfg,gy->kfy", prod_real, sin_core, precision=PRECISE) + jnp.einsum(
        "kfg,gy->kfy", prod_imag, cos_core, precision=PRECISE
    )
    field_real = jnp.einsum("fx,kfy->kxy", cos_core, half_real, precision=PRECISE) - jnp.einsum(
        "fx,kfy->kxy", sin_core, half_imag, precision=PRECISE
    )
    field_imag = jnp.einsum("fx,kfy->kxy", cos_core, half_imag, precision=PRECISE) + jnp.einsum(
        "fx,kfy->kxy", sin_core, half_real, precision=PRECISE
    )
    intensity = jnp.sum(
        weights[:, None, None] * (field_real * field_real + field_imag * field_imag), axis=0
    )
    resist = jax.nn.sigmoid(STEEPNESS * (dose * intensity - THRESHOLD))
    missed = resist - target_tile
    return jnp.sum(missed * missed)


def shards(latent, target, kernel_table, socs_weights, dose_levels, cond_focus, cond_dose):
    group_rows = latent.shape[0]
    tile_devices = lax.axis_size("tile")
    cond_devices = lax.axis_size("cond")
    region_rows = group_rows * cond_devices
    pixel_count = region_rows * TILE
    cond_count = cond_focus.shape[0]
    focus_levels = jnp.arange(kernel_table.shape[0], dtype=jnp.int32)
    focus_hot = (cond_focus[:, None] == focus_levels[None, :]).astype(jnp.float32)
    spectra_all = jnp.einsum("cf,fkrab->ckrab", focus_hot, kernel_table, precision=PRECISE)
    dose_indices = jnp.arange(dose_levels.shape[0], dtype=jnp.int32)
    dose_hot = (cond_dose[:, None] == dose_indices[None, :]).astype(jnp.float32)
    dose_all = jnp.sum(dose_hot * dose_levels[None, :], axis=1)
    cos_full, sin_full = make_tables(NF, EXT, 0, EXT)
    cos_core, sin_core = make_tables(NF, EXT, HALO, TILE)
    tables = (cos_full, sin_full, cos_core, sin_core)
    wide = lax.all_gather(latent, "tile", axis=1, tiled=True)
    cond_part = cond_count // tile_devices
    cond_start = lax.axis_index("tile") * cond_part
    row_begin = lax.axis_index("cond") * group_rows
    padded = with_halo(jax.nn.sigmoid(wide), (("cond", 0),), HALO)
    targets = (
        lax.dynamic_slice_in_dim(target, row_begin, group_rows, 0)
        .astype(jnp.float32)
        .reshape(-1, TILE, TILE)
    )
    my_spectra = lax.dynamic_slice_in_dim(spectra_all, cond_start, cond_part, 0)
    my_dose = lax.dynamic_slice_in_dim(dose_all, cond_start, cond_part, 0)
    tile_ids = jnp.arange(targets.shape[0], dtype=jnp.int32)
    anchor = jnp.int32(0)

    def cond_error(packed):
        spectra, dose = packed

        def one_tile(index):
            tile_block = lax.dynamic_slice(padded, (index * TILE, anchor), (EXT, TILE))
            target_tile = lax.dynamic_index_in_dim(targets, index, 0, keepdims=False)
            return tile_error(tile_block, spectra, socs_weights, dose, target_tile, tables)

        return jnp.sum(lax.map(one_tile, tile_ids))

    partial_errors = lax.map(cond_error, (my_spectra, my_dose))
    totals = lax.psum(partial_errors, "cond")
    exponent = jnp.exp(SHARPNESS * totals / pixel_count)
    denominator = lax.psum(jnp.sum(exponent), "tile")
    cond_weights = exponent / denominator
    worst_loss = (jnp.log(denominator) / SHARPNESS).reshape(1)

    def advance(gradient, index):
        row_start = index * TILE
        tile_block = lax.dynamic_slice(padded, (row_start, anchor), (EXT, TILE))
        target_tile = lax.dynamic_index_in_dim(targets, index, 0, keepdims=False)

        def cond_grad(packed):
            spectra, dose, weight = packed
            _, pullback = jax.vjp(
                lambda blocked: tile_error(
                    blocked, spectra, socs_weights, dose, target_tile, tables
                ),
                tile_block,
            )
            return pullback(weight)[0]

        increment = jnp.sum(lax.map(cond_grad, (my_spectra, my_dose, cond_weights)), axis=0)
        current = lax.dynamic_slice(gradient, (row_start, anchor), (EXT, TILE))
        return (lax.dynamic_update_slice(gradient, current + increment, (row_start, anchor)), None)

    gradient, _ = lax.scan(advance, jnp.zeros(padded.shape, jnp.float32), tile_ids)
    overflow = jnp.concatenate([gradient[:HALO], gradient[-HALO:]], axis=0)
    beside_all = with_halo(overflow, (("cond", 0),), HALO)
    central = gradient[HALO : HALO + group_rows]
    central = central.at[:HALO].add(beside_all[:HALO])
    central = central.at[group_rows - HALO :].add(beside_all[3 * HALO :])
    own_rows = lax.psum_scatter(central, "tile", scatter_dimension=1, tiled=True)
    mask_own = jax.nn.sigmoid(latent)
    mask_gradient = GRAD_GAIN * own_rows * (mask_own * (1.0 - mask_own))
    return (mask_gradient, worst_loss)


def solution(mesh):
    in_specs = (P(("grp", "cond"), "tile"), P("grp", None), P(), P(), P(), P(), P())
    out_specs = (P(("grp", "cond"), "tile"), P("grp"))
    return jax.shard_map(shards, mesh=mesh, in_specs=in_specs, out_specs=out_specs, check_vma=False)
```

profile of v0, /device:TPU:0, one launch (start us, length us, event | category | flops | bytes accessed | tf_op | source)
XLA Modules:
  0.0 336.7 jit_solution(5229314790434188424)
XLA Ops:
  7.2 2.2 all_gather.3
  9.5 4.8 %collective-permute-start = (f32[16,128]{0,1:T(8,128)S(1)}, f32[16,128]{0,1:T(8,128)S(1)}, u32[]{:S(2)}, u32[]{:S(2)}) collective-permute-start(f32[16,128]{0,1:T(8,128)S(1)} %get-tuple-element.1472), channel_id=1, source_target_pairs={{0,1},{1,2},{2,3},{3,4},{4,5},{5,6},{6,7},{8,9},{9,10},{10,11},{11... | collective-permute-start | bytes 24584 | tf_op jit(solution)/shard_map/ppermute | solution.py:29
  14.3 1.3 collective-permute-start.1
  15.6 5.4 %fusion.171 = f32[8,8,2,65,65]{4,0,3,2,1:T(8,128)S(1)} fusion(f32[8,8,2,65,65]{4,2,3,1,0:T(2,128)} %param.21, s32[8]{0:T(128)} %param.24), kind=kOutput, calls=%fused_computation.203 | convolution fusion | flops 51916864 | bytes 4326432 | tf_op jit(solution)/shard_map/cf,fkrab->ckrab/dot_general | solution.py:90
  22.7 1.6 copy.60
  24.8 113.7 %while.79 = (s32[]{:T(128)}, f32[4]{0:T(128)S(1)}, f32[4,8,2,65,65]{4,3,1,2,0:T(8,128)}, f32[4]{0:T(128)S(1)}, f32[8]{0:T(128)S(1)}, /*index=5*/f32[288,128]{1,0...) while((s32[]{:T(128)}, f32[4]{0:T(128)S(1)}, ...), condition=%wide.region_7.8_spmd.clone.clone.clone, body=%wide.region_1.7_spmd.clone.clone.clone.sunk | while | flops 682918464 | bytes 9002610 | solution.py:122
  24.8 1.1 dynamic-slice_bitcast_fusion.6
  27.1 24.7 %while.82 = (s32[]{:T(128)}, f32[2]{0:T(128)S(1)}, f32[]{:T(128)}, f32[8]{0:T(128)S(1)}, f32[8,2,65,65]{3,2,0,1:T(8,128)S(1)}, /*index=5*/s32[2]{0:T(128)S(1)}, ...) while((s32[]{:T(128)}, f32[2]{0:T(128)S(1)}, f32[]{:T(128)}, ...), condition=%wide.region_5.5_spmd.clone, body=%wide.region_2.4_spmd.clone.sunk | while | flops 682749952 | bytes 8310657 | solution.py:120
  34.7 1.0 fusion.440
  37.6 1.2 fusion.441
  47.1 1.0 fusion.440
  49.9 1.2 fusion.441
  53.2 1.1 dynamic-slice_bitcast_fusion.6
  55.6 24.7 %while.82 = (s32[]{:T(128)}, f32[2]{0:T(128)S(1)}, f32[]{:T(128)}, f32[8]{0:T(128)S(1)}, f32[8,2,65,65]{3,2,0,1:T(8,128)S(1)}, /*index=5*/s32[2]{0:T(128)S(1)}, ...) while((s32[]{:T(128)}, f32[2]{0:T(128)S(1)}, f32[]{:T(128)}, ...), condition=%wide.region_5.5_spmd.clone, body=%wide.region_2.4_spmd.clone.sunk | while | flops 682749952 | bytes 8310657 | solution.py:120
  63.1 1.0 fusion.440
  66.0 1.2 fusion.441
  75.5 1.0 fusion.440
  78.4 1.2 fusion.441
  81.7 1.1 dynamic-slice_bitcast_fusion.6
  84.0 24.7 %while.82 = (s32[]{:T(128)}, f32[2]{0:T(128)S(1)}, f32[]{:T(128)}, f32[8]{0:T(128)S(1)}, f32[8,2,65,65]{3,2,0,1:T(8,128)S(1)}, /*index=5*/s32[2]{0:T(128)S(1)}, ...) while((s32[]{:T(128)}, f32[2]{0:T(128)S(1)}, f32[]{:T(128)}, ...), condition=%wide.region_5.5_spmd.clone, body=%wide.region_2.4_spmd.clone.sunk | while | flops 682749952 | bytes 8310657 | solution.py:120
  91.6 1.0 fusion.440
  94.4 1.2 fusion.441
  103.9 1.0 fusion.440
  106.8 1.2 fusion.441
  110.1 1.1 dynamic-slice_bitcast_fusion.6
  112.4 24.7 %while.82 = (s32[]{:T(128)}, f32[2]{0:T(128)S(1)}, f32[]{:T(128)}, f32[8]{0:T(128)S(1)}, f32[8,2,65,65]{3,2,0,1:T(8,128)S(1)}, /*index=5*/s32[2]{0:T(128)S(1)}, ...) while((s32[]{:T(128)}, f32[2]{0:T(128)S(1)}, f32[]{:T(128)}, ...), condition=%wide.region_5.5_spmd.clone, body=%wide.region_2.4_spmd.clone.sunk | while | flops 682749952 | bytes 8310657 | solution.py:120
  120.0 1.0 fusion.440
  122.9 1.2 fusion.441
  132.3 1.0 fusion.440
  135.2 1.2 fusion.441
  138.5 22.8 %psum.14 = f32[4]{0:T(128)S(1)} all-reduce(f32[4]{0:T(128)S(1)} %get-tuple-element.2042), channel_id=1, replica_groups=mesh['grp'=2,'tile'=2,'cond'=8] {'cond'}, use_global_device_ids=true, to_apply=%region_8.9 | all-reduce | flops 4 | bytes 32 | tf_op jit(solution)/shard_map/psum | solution.py:123
  161.9 3.1 psum.15
  165.7 146.4 %while.81 = (s32[]{:T(128)}, f32[288,128]{1,0:T(8,128)S(1)}, s32[2]{0:T(128)S(1)}, f32[2,128,128]{1,2,0:T(8,128)S(1)}, f32[288,128]{1,0:T(8,128)S(1)}, /*index=5...) while((s32[]{:T(128)}, f32[288,128]{1,0:T(8,128)S(1)}, ...), condition=%wide.region_20.21_spmd.clone.clone.clone, body=%wide.region_11.20_spmd.clone.clone.clone.sunk | while | flops 1366997760 | bytes 17561488 | solution.py:148
  172.7 66.2 %while.83 = (s32[]{:T(128)}, f32[4,160,128]{2,1,0:T(8,128)S(1)}, f32[4,8,2,65,65]{4,3,1,2,0:T(8,128)}, f32[65,65]{1,0:T(8,128)S(1)}, f32[65,65]{1,0:T(8,128)S(1)...) while((s32[]{:T(128)}, f32[4,160,128]{2,1,0:T(8,128)S(1)}, ...), condition=%wide.region_18.18_spmd.clone, body=%wide.region_12.17_spmd.clone.sunk | while | flops 1301807488 | bytes 16038325 | solution.py:144
  172.7 1.1 dynamic-slice_bitcast_fusion.8
  178.5 1.0 multiply_reduce_fusion.7
  181.3 1.3 fusion.389
  189.3 1.1 dynamic-slice_bitcast_fusion.8
  195.0 1.0 multiply_reduce_fusion.7
  197.9 1.3 fusion.389
  205.9 1.1 dynamic-slice_bitcast_fusion.8
  211.6 1.0 multiply_reduce_fusion.7
  214.4 1.3 fusion.389
  222.4 1.1 dynamic-slice_bitcast_fusion.8
  228.1 1.0 multiply_reduce_fusion.7
  231.0 1.3 fusion.389
  245.9 66.2 %while.83 = (s32[]{:T(128)}, f32[4,160,128]{2,1,0:T(8,128)S(1)}, f32[4,8,2,65,65]{4,3,1,2,0:T(8,128)}, f32[65,65]{1,0:T(8,128)S(1)}, f32[65,65]{1,0:T(8,128)S(1)...) while((s32[]{:T(128)}, f32[4,160,128]{2,1,0:T(8,128)S(1)}, ...), condition=%wide.region_18.18_spmd.clone, body=%wide.region_12.17_spmd.clone.sunk | while | flops 1301807488 | bytes 16038325 | solution.py:144
  245.9 1.1 dynamic-slice_bitcast_fusion.8
  251.6 1.0 multiply_reduce_fusion.7
  254.4 1.3 fusion.389
  262.4 1.1 dynamic-slice_bitcast_fusion.8
  268.2 1.0 multiply_reduce_fusion.7
  271.0 1.3 fusion.389
  279.0 1.1 dynamic-slice_bitcast_fusion.8
  284.7 1.0 multiply_reduce_fusion.7
  287.6 1.3 fusion.389
  295.5 1.1 dynamic-slice_bitcast_fusion.8
  301.3 1.0 multiply_reduce_fusion.7
  304.1 1.3 fusion.389
  312.3 1.3 collective-permute-start.2
  313.7 1.3 collective-permute-start.3
  316.2 3.6 %collective-permute-done.3 = f32[16,128]{0,1:T(8,128)S(1)} collective-permute-done((f32[16,128]{0,1:T(8,128)S(1)}, f32[16,128]{0,1:T(8,128)S(1)}, u32[]{:S(2)}, u32[]{:S(2)}) %collective-permute-start.3) | collective-permute-done | bytes 8224 | tf_op jit(solution)/shard_map/ppermute | solution.py:31
  321.9 5.4 %reduce-scatter.2.cloned.1.call-done = f32[256,64]{0,1:T(8,128)} async-done(((f32[256,128]{0,1:T(8,128)}), f32[256,64]{0,1:T(8,128)}) %reduce-scatter.2.cloned.1.call-update) | async-done | bytes 65552 | tf_op jit(solution)/shard_map/reduce_scatter | solution.py:154
  327.3 1.5 fusion.173
  (419 shorter events, 185.3 us)
Async XLA Ops:
  7.2 320.1 %reduce-scatter.2.cloned.1.call-start = ((), (), s32[]{:S(2)}) async-start(), calls=%async_computation.1 | async-start | bytes 196608 | tf_op jit(solution)/shard_map/reduce_scatter | solution.py:154
  9.5 15.0 %collective-permute-start = (f32[16,128]{0,1:T(8,128)S(1)}, f32[16,128]{0,1:T(8,128)S(1)}, u32[]{:S(2)}, u32[]{:S(2)}) collective-permute-start(f32[16,128]{0,1:T(8,128)S(1)} %get-tuple-element.1472), channel_id=1, source_target_pairs={{0,1},{1,2},{2,3},{3,4},{4,5},{5,6},{6,7},{8,9},{9,10},{10,11},{11... | collective-permute-start | bytes 24584 | tf_op jit(solution)/shard_map/ppermute | solution.py:29
  14.3 10.2 %collective-permute-start.1 = (f32[16,128]{0,1:T(8,128)S(1)}, f32[16,128]{0,1:T(8,128)S(1)}, u32[]{:S(2)}, u32[]{:S(2)}) collective-permute-start(f32[16,128]{0,1:T(8,128)S(1)} %get-tuple-element.1473), channel_id=1, source_target_pairs={{1,0},{2,1},{3,2},{4,3},{5,4},{6,5},{7,6},{9,8},{10,9},{11,10},{12... | collective-permute-start | bytes 24584 | tf_op jit(solution)/shard_map/ppermute | solution.py:31
  21.0 0.7 copy-start.3
  21.1 0.7 copy-start.4
  21.1 3.7 %copy-start = (f32[8]{0:T(128)S(1)}, f32[8]{0:T(128)}, u32[]{:S(2)}) copy-start(f32[8]{0:T(128)} %param.22) | copy-start | bytes 100
  165.7 161.6 %copy-start.2 = (f32[256,64]{0,1:T(8,128)S(1)}, f32[256,64]{0,1:T(8,128)}, u32[]{:S(2)}) copy-start(f32[256,64]{0,1:T(8,128)} %param.19) | copy-start | bytes 196612
  312.3 3.2 collective-permute-start.2
  313.7 6.2 %collective-permute-start.3 = (f32[16,128]{0,1:T(8,128)S(1)}, f32[16,128]{0,1:T(8,128)S(1)}, u32[]{:S(2)}, u32[]{:S(2)}) collective-permute-start(f32[16,128]{0,1:T(8,128)S(1)} %copy.64), channel_id=1, source_target_pairs={{1,0},{2,1},{3,2},{4,3},{5,4},{6,5},{7,6},{9,8},{10,9},{11,10},{12... | collective-permute-start | bytes 24584 | tf_op jit(solution)/shard_map/ppermute | solution.py:31
  320.5 0.6 copy-start.1
Sparse Core Ops, SparseCore 0:
  321.3 5.9 reduce-scatter.1
where the time goes:
time: 338 us; the launch traced here: 337 us
  matrix products  165 us (49%)
  local copies, waits for them, and re-layouts  47.4 us (14%)
  loops' own time  31.7 us (9%)
  other arithmetic  30.1 us (9%)
  blocking collectives  28.1 us (8%)
  between operations  16.1 us (5%)
  waiting for transfers between devices  9.28 us (3%)
  starting transfers between devices  8.67 us (3%)
    psum x1, blocking collectives, shards(): totals = lax.psum(partial_errors, 'cond')  22.8 us
    dot_general x24, matrix products, tile_error(): jnp.einsum('fx,kfy->kxy', sin_core, half_real, precision=PRECISE)  22.5 us
    dot_general x24, matrix products, tile_error(): jnp.einsum('fx,kfy->kxy', sin_core, half_imag, precision=PRECISE)  22.5 us
    dot_general x24, matrix products, tile_error(): jnp.einsum('fx,kfy->kxy', cos_core, half_real, precision=PRECISE)  22.4 us
    dot_general x24, matrix products, tile_error(): jnp.einsum('fx,kfy->kxy', cos_core, half_imag, precision=PRECISE)  22.4 us
    another operation x4, loops' own time, cond_error(): return jnp.sum(lax.map(one_tile, tile_ids))  20.9 us
    squeeze x12, local copies, waits for them, and re-layouts, shards(): partial_errors = lax.map(cond_error, (my_spectra, my_dose))  13.3 us
    dynamic_slice x20, local copies, waits for them, and re-layouts, shards(): partial_errors = lax.map(cond_error, (my_spectra, my_dose))  12.3 us
  transfers between devices with their start and end apart: 5, of which 3 were waited for; matrix products, arithmetic and copies ran while one was open for 3% of the time, Pallas kernels for 0%

commit v1 on v0

v1 whole, which is shorter than its diff:
```python
import functools
import math

import jax
import jax.numpy as jnp
import ml_dtypes
import numpy as np
from jax import lax
from jax.experimental import pallas as pl
from jax.experimental.pallas import tpu as pltpu
from jax.sharding import PartitionSpec as P

TILE = 128
HALO = 16
NF = 65
EXT = 160
FP = 80
GP = 128

STEEPNESS = 4.0
THRESHOLD = 1.0
SHARPNESS = 6.0
GRAD_GAIN = 256.0
MESH = pl.DeviceIdType.MESH
BF = jnp.bfloat16


def halves(table):
    high = table.astype(np.float32).astype(ml_dtypes.bfloat16)
    low = (table - high.astype(np.float64)).astype(np.float32).astype(ml_dtypes.bfloat16)
    return high, low


def left_table(table):
    high, low = halves(table)
    return np.concatenate([high, high, low], axis=1)


def right_table(table):
    high, low = halves(table)
    return np.concatenate([high, high, low], axis=0)


def make_tables(parts):
    freq = np.arange(NF) - (NF - 1) // 2

    def waves(positions, rows):
        phase = 2.0 * math.pi * ((freq[:, None] * positions[None, :]) % EXT) / EXT
        pad = ((0, rows - NF), (0, 0))
        return np.pad(np.cos(phase), pad), np.pad(np.sin(phase), pad)

    core = np.arange(TILE) + HALO
    cos_full, sin_full = waves(np.arange(EXT), FP)
    cos_rows, sin_rows = waves(core, FP)
    cos_lane, sin_lane = waves(core, GP)
    width = TILE // parts
    cols = np.concatenate([cos_lane.T, -sin_lane.T], axis=1)
    col_halves = [cols[h * width : (h + 1) * width] for h in range(parts)]
    col_high = np.stack([halves(c)[0] for c in col_halves])
    col_low = np.stack([halves(c)[1] for c in col_halves])
    col_back = np.stack([right_table(c.T) for c in col_halves])
    spec = np.block([[cos_full, sin_full], [-sin_full, cos_full]])
    rows = np.block([[cos_rows.T, -sin_rows.T], [sin_rows.T, cos_rows.T]])
    field = np.block([[cos_lane, sin_lane], [-sin_lane, cos_lane]])
    return (
        col_high,
        col_low,
        col_back,
        left_table(spec),
        left_table(spec.T),
        left_table(rows),
        left_table(rows.T),
        right_table(field),
        right_table(field.T),
    )


def split(values):
    high = values.astype(BF)
    low = (values - high.astype(jnp.float32)).astype(BF)
    return high, low


def mul(a, b):
    return jnp.dot(a, b, preferred_element_type=jnp.float32)


def data_left(values, table):
    high, low = split(values)
    return mul(jnp.concatenate([high, low, high], axis=1), table)


def data_right(table, values):
    high, low = split(values)
    return mul(table, jnp.concatenate([high, low, high], axis=0))


def kernel(
    sizes,
    latent_ref,
    target_hbm,
    table_hbm,
    socs_ref,
    dose_ref,
    focus_ref,
    level_ref,
    col_high,
    col_low,
    col_back,
    spec_tab,
    spec_back,
    row_tab,
    row_back,
    field_tab,
    field_back,
    grad_out,
    loss_out,
    mask,
    raw,
    kern,
    target,
    spec,
    field,
    slope,
    dspec,
    grad,
    peer_grad,
    upper,
    lower,
    errors,
    local_sem,
    mask_send,
    mask_recv,
    err_send,
    err_recv,
    grad_send,
    grad_recv,
):
    parts, groups, rows, conds, kernels, pixels, all_conds, doses = sizes
    g = lax.axis_index("grp")
    j = lax.axis_index("tile")
    i = lax.axis_index("cond")
    tiles = rows // TILE
    me = i * parts + j
    everyone = parts * groups
    inverse_area = 1.0 / (EXT * EXT)

    table_copy = pltpu.make_async_copy(
        table_hbm.at[pl.ds(j * conds, conds)], raw, local_sem.at[0]
    )
    table_copy.start()
    target_copy = pltpu.make_async_copy(
        target_hbm.at[pl.ds(i * rows, rows)], target, local_sem.at[1]
    )
    target_copy.start()

    errors[j, i] = jnp.zeros(errors.shape[2:], jnp.float32)
    upper[...] = jnp.zeros_like(upper)
    lower[...] = jnp.zeros_like(lower)

    barrier = pltpu.get_barrier_semaphore()

    def greet(step, carry):
        other = (me + step) % everyone
        pl.semaphore_signal(
            barrier, inc=1, device_id=(g, other % parts, other // parts), device_id_type=MESH
        )
        return carry

    lax.fori_loop(1, everyone, greet, 0)

    mask_own = jax.nn.sigmoid(latent_ref[...])
    mask[j, HALO : HALO + rows, :] = mask_own
    grad[...] = jnp.zeros_like(grad)

    @pl.when(i == 0)
    def _():
        for h in range(parts):
            mask[h, 0:HALO, :] = jnp.zeros((HALO, TILE // parts), jnp.float32)

    @pl.when(i == groups - 1)
    def _():
        for h in range(parts):
            mask[h, HALO + rows :, :] = jnp.zeros((HALO, TILE // parts), jnp.float32)

    pl.semaphore_wait(barrier, everyone - 1)

    def mask_peer(d):
        block = mask.at[j, pl.ds(HALO, rows)]
        return pltpu.make_async_remote_copy(
            block, block, mask_send.at[d], mask_recv.at[d],
            device_id=(g, (j + d) % parts, i), device_id_type=MESH,
        )

    def mask_edge(up, d):
        src = mask.at[j, pl.ds(HALO, HALO)] if up else mask.at[j, pl.ds(rows, HALO)]
        dst = mask.at[j, pl.ds(HALO + rows, HALO)] if up else mask.at[j, pl.ds(0, HALO)]
        slot = parts + (0 if up else parts) + d
        return pltpu.make_async_remote_copy(
            src, dst, mask_send.at[slot], mask_recv.at[slot],
            device_id=(g, (j + d) % parts, i - 1 if up else i + 1), device_id_type=MESH,
        )

    for d in range(1, parts):
        mask_peer(d).start()

    @pl.when(i > 0)
    def _():
        for d in range(parts):
            mask_edge(True, d).start()

    @pl.when(i < groups - 1)
    def _():
        for d in range(parts):
            mask_edge(False, d).start()

    table_copy.wait()
    kern[...] = jnp.zeros_like(kern)

    def pad_kernels(c, carry):
        for k in range(kernels):
            for part in range(2):
                kern[c, k, part, 0:NF, 0:NF] = raw[c, k, part]
        return carry

    lax.fori_loop(0, conds, pad_kernels, 0)

    target_copy.wait()

    for d in range(1, parts):
        mask_peer(d).wait()

    @pl.when(i > 0)
    def _():
        for d in range(parts):
            mask_edge(True, d).wait_send()
            mask_edge(False, d).wait_recv()

    @pl.when(i < groups - 1)
    def _():
        for d in range(parts):
            mask_edge(False, d).wait_send()
            mask_edge(True, d).wait_recv()

    for t in range(tiles):
        cols = None
        for h in range(parts):
            high, low = split(mask[h, t * TILE : t * TILE + EXT, :])
            term = mul(high, col_high[h]) + mul(low, col_high[h]) + mul(high, col_low[h])
            cols = term if cols is None else cols + term
        stacked = jnp.concatenate([cols[:, :GP], cols[:, GP:]], axis=0)
        spec[t] = data_right(spec_tab[...], stacked) * inverse_area

    cond_doses = []
    for c in range(all_conds):
        value = jnp.float32(0.0)
        for n in range(doses):
            value = jnp.where(level_ref[c] == n, dose_ref[n], value)
        cond_doses.append(value)

    def forward(index, carry):
        c = index // tiles
        t = index % tiles
        dose = jnp.float32(0.0)
        for n in range(all_conds):
            dose = jnp.where(focus_ref[n] == j * conds + c, cond_doses[n], dose)
        spec_real = spec[t, 0:FP, :]
        spec_imag = spec[t, FP:, :]
        columns = []
        for k in range(kernels):
            kern_real = kern[c, k, 0]
            kern_imag = kern[c, k, 1]
            prod = jnp.concatenate(
                [
                    kern_real * spec_real - kern_imag * spec_imag,
                    kern_real * spec_imag + kern_imag * spec_real,
                ],
                axis=0,
            )
            high, low = split(prod)
            columns.append(jnp.concatenate([high, low, high], axis=0))
        half = mul(row_tab[...], jnp.concatenate(columns, axis=1))
        left = []
        for k in range(kernels):
            part = half[:, k * GP : (k + 1) * GP]
            high, low = split(jnp.concatenate([part[:TILE], part[TILE:]], axis=1))
            left.append(jnp.concatenate([high, low, high], axis=1))
        image = mul(jnp.concatenate(left, axis=0), field_tab[...])
        field[index] = image
        intensity = jnp.zeros((TILE, TILE), jnp.float32)
        for k in range(kernels):
            part = image[k * TILE : (k + 1) * TILE]
            real, imag = part[:, :TILE], part[:, TILE:]
            intensity = intensity + socs_ref[k] * (real * real + imag * imag)
        resist = jax.nn.sigmoid(STEEPNESS * (dose * intensity - THRESHOLD))
        wanted = target[pl.ds(pl.multiple_of(t * TILE, TILE), TILE), :].astype(jnp.float32)
        missed = resist - wanted
        slope[index] = (4.0 * STEEPNESS) * dose * (missed * (resist * (1.0 - resist)))
        sums = jnp.sum(missed * missed, axis=0, keepdims=True)
        errors[j, i, pl.ds(c, 1), :] = errors[j, i, pl.ds(c, 1), :] + sums
        return carry

    lax.fori_loop(0, conds * tiles, forward, 0)

    def err_copy(step):
        other = (me + step) % everyone
        block = errors.at[j, i]
        return pltpu.make_async_remote_copy(
            block, block, err_send.at[step], err_recv.at[step],
            device_id=(g, other % parts, other // parts), device_id_type=MESH,
        )

    def send_error(step, carry):
        err_copy(step).start()
        return carry

    lax.fori_loop(1, everyone, send_error, 0)

    def backward(index, carry):
        c = index // tiles
        t = index % tiles
        gain = slope[index]
        left = []
        for k in range(kernels):
            part = field[index, k * TILE : (k + 1) * TILE, :]
            scale = socs_ref[k] * gain
            high, low = split(
                jnp.concatenate([part[:, :TILE] * scale, part[:, TILE:] * scale], axis=1)
            )
            left.append(jnp.concatenate([high, low, high], axis=1))
        half = mul(jnp.concatenate(left, axis=0), field_back[...])
        columns = []
        for k in range(kernels):
            part = half[k * TILE : (k + 1) * TILE]
            high, low = split(jnp.concatenate([part[:, :GP], part[:, GP:]], axis=0))
            columns.append(jnp.concatenate([high, low, high], axis=0))
        prod = mul(row_back[...], jnp.concatenate(columns, axis=1))
        real = jnp.zeros((FP, GP), jnp.float32)
        imag = jnp.zeros((FP, GP), jnp.float32)
        for k in range(kernels):
            prod_real = prod[:FP, k * GP : (k + 1) * GP]
            prod_imag = prod[FP:, k * GP : (k + 1) * GP]
            kern_real = kern[c, k, 0]
            kern_imag = kern[c, k, 1]
            real = real + (kern_real * prod_real + kern_imag * prod_imag)
            imag = imag + (kern_real * prod_imag - kern_imag * prod_real)
        dspec[index, 0:FP, :] = real
        dspec[index, FP:, :] = imag
        return carry

    lax.fori_loop(0, conds * tiles, backward, 0)

    def wait_error(step, carry):
        err_copy(step).wait()
        return carry

    lax.fori_loop(1, everyone, wait_error, 0)

    slots = errors.shape[2]
    valid = lax.broadcasted_iota(jnp.int32, (slots, 1), 0) < conds
    denominator = jnp.zeros((1, 1), jnp.float32)
    mine = jnp.zeros((slots, 1), jnp.float32)
    for h in range(parts):
        total = errors[h, 0]
        for n in range(1, groups):
            total = total + errors[h, n]
        score = SHARPNESS * jnp.sum(total, axis=1, keepdims=True) / pixels
        exponent = jnp.where(valid, jnp.exp(score), 0.0)
        denominator = denominator + jnp.sum(exponent, axis=0, keepdims=True)
        mine = jnp.where(j == h, exponent, mine)
    weights = mine / denominator
    loss_out[...] = jnp.broadcast_to(jnp.log(denominator) / SHARPNESS, loss_out.shape)

    for t in range(tiles):
        total = jnp.zeros((2 * FP, GP), jnp.float32)
        for c in range(conds):
            total = total + weights[c : c + 1, :] * dspec[c * tiles + t]
        stacked = data_right(spec_back[...], total * inverse_area)
        wide = jnp.concatenate([stacked[:EXT], stacked[EXT:]], axis=1)
        high, low = split(wide)
        left = jnp.concatenate([high, low, high], axis=1)
        for h in range(parts):
            window = (h, slice(t * TILE, t * TILE + EXT), slice(None))
            grad[window] = grad[window] + mul(left, col_back[h])

    def grad_peer(d):
        return pltpu.make_async_remote_copy(
            grad.at[(j + d) % parts, pl.ds(HALO, rows)], peer_grad.at[d - 1],
            grad_send.at[d], grad_recv.at[d],
            device_id=(g, (j + d) % parts, i), device_id_type=MESH,
        )

    def grad_edge(up, d):
        to = (j + d) % parts
        src = grad.at[to, pl.ds(0, HALO)] if up else grad.at[to, pl.ds(HALO + rows, HALO)]
        dst = lower.at[d] if up else upper.at[d]
        slot = parts + (0 if up else parts) + d
        return pltpu.make_async_remote_copy(
            src, dst, grad_send.at[slot], grad_recv.at[slot],
            device_id=(g, to, i - 1 if up else i + 1), device_id_type=MESH,
        )

    @pl.when(i > 0)
    def _():
        for d in range(parts):
            grad_edge(True, d).start()

    @pl.when(i < groups - 1)
    def _():
        for d in range(parts):
            grad_edge(False, d).start()

    for d in range(1, parts):
        grad_peer(d).start()

    own = mask[j, HALO : HALO + rows, :]
    scale = GRAD_GAIN * (own * (1.0 - own))
    total = grad[j, HALO : HALO + rows, :]

    for d in range(1, parts):
        grad_peer(d).wait()
        total = total + peer_grad[d - 1]

    @pl.when(i > 0)
    def _():
        for d in range(parts):
            grad_edge(True, d).wait_send()
            grad_edge(False, d).wait_recv()

    @pl.when(i < groups - 1)
    def _():
        for d in range(parts):
            grad_edge(False, d).wait_send()
            grad_edge(True, d).wait_recv()

    head, tail = upper[0], lower[0]
    for d in range(1, parts):
        head = head + upper[d]
        tail = tail + lower[d]
    grad_out[...] = total * scale
    grad_out[0:HALO, :] = (total[0:HALO] + head) * scale[0:HALO]
    grad_out[rows - HALO :, :] = (total[rows - HALO :] + tail) * scale[rows - HALO :]


def shards(latent, target, kernel_table, socs_weights, dose_levels, cond_focus, cond_dose):
    parts = lax.axis_size("tile")
    groups = lax.axis_size("cond")
    rows, width = latent.shape
    kernels = kernel_table.shape[1]
    all_conds = cond_focus.shape[0]
    conds = all_conds // parts
    tiles = rows // TILE
    pixels = rows * groups * TILE
    tables = [jnp.asarray(table) for table in make_tables(parts)]
    sizes = (parts, groups, rows, conds, kernels, pixels, all_conds, dose_levels.shape[0])
    slots = -(-conds // 8) * 8
    vmem = pl.BlockSpec(memory_space=pltpu.VMEM)
    smem = pl.BlockSpec(memory_space=pltpu.SMEM)
    anywhere = pl.BlockSpec(memory_space=pl.ANY)
    f32 = jnp.float32
    everyone = parts * groups
    mask_gradient, loss = pl.pallas_call(
        functools.partial(kernel, sizes),
        out_shape=(
            jax.ShapeDtypeStruct((rows, width), f32),
            jax.ShapeDtypeStruct((8, 128), f32),
        ),
        in_specs=[vmem, anywhere, anywhere, smem, smem, smem, smem] + [vmem] * len(tables),
        out_specs=(vmem, vmem),
        scratch_shapes=[
            pltpu.VMEM((parts, rows + 2 * HALO, width), f32),
            pltpu.VMEM((conds,) + kernel_table.shape[1:], f32),
            pltpu.VMEM((conds, kernels, 2, FP, GP), f32),
            pltpu.VMEM((rows, TILE), jnp.int32),
            pltpu.VMEM((tiles, 2 * FP, GP), f32),
            pltpu.VMEM((conds * tiles, kernels * TILE, 2 * TILE), f32),
            pltpu.VMEM((conds * tiles, TILE, TILE), f32),
            pltpu.VMEM((conds * tiles, 2 * FP, GP), f32),
            pltpu.VMEM((parts, rows + 2 * HALO, width), f32),
            pltpu.VMEM((max(parts - 1, 1), rows, width), f32),
            pltpu.VMEM((parts, HALO, width), f32),
            pltpu.VMEM((parts, HALO, width), f32),
            pltpu.VMEM((parts, groups, slots, TILE), f32),
            pltpu.SemaphoreType.DMA((2,)),
            pltpu.SemaphoreType.DMA((3 * parts,)),
            pltpu.SemaphoreType.DMA((3 * parts,)),
            pltpu.SemaphoreType.DMA((everyone,)),
            pltpu.SemaphoreType.DMA((everyone,)),
            pltpu.SemaphoreType.DMA((3 * parts,)),
            pltpu.SemaphoreType.DMA((3 * parts,)),
        ],
        compiler_params=pltpu.CompilerParams(
            collective_id=0, has_side_effects=True, vmem_limit_bytes=56 * 1024 * 1024
        ),
        name="litho",
    )(
        latent, target, kernel_table, socs_weights, dose_levels, cond_focus, cond_dose, *tables
    )
    return (mask_gradient, loss[0, :1])


def solution(mesh):
    in_specs = (P(("grp", "cond"), "tile"), P("grp", None), P(), P(), P(), P(), P())
    out_specs = (P(("grp", "cond"), "tile"), P("grp"))
    return jax.shard_map(shards, mesh=mesh, in_specs=in_specs, out_specs=out_specs, check_vma=False)
```

time: 338 us -> 44.7 us (0.13)
  matrix products: 165 us -> 0 us
  local copies, waits for them, and re-layouts: 47.4 us -> 9.21 us
  Pallas kernels: 0 us -> 34.6 us
  loops' own time: 31.7 us -> 0 us
  other arithmetic: 30.1 us -> 0 us
  blocking collectives: 28.1 us -> 0 us
  between operations: 16.1 us -> 0.64 us
  waiting for transfers between devices: 9.28 us -> 0 us
  starting transfers between devices: 8.67 us -> 0 us
    dot_general x301 -> x0, matrix products: 165 us -> none  [the longest x24 22.5 us: tile_error(): jnp.einsum('fx,kfy->kxy', sin_core, half_real, precision=PRECISE)]
    pallas_call x0 -> x1, Pallas kernels: none -> 34.6 us  [shards(): pl.pallas_call(functools.partial(kernel, sizes), out_shape=(jax.ShapeDtyp...]
    another operation x8 -> x0, loops' own time: 31.7 us -> none  [the longest x4 20.9 us: cond_error(): return jnp.sum(lax.map(one_tile, tile_ids))]
    psum x2 -> x0, blocking collectives: 25.9 us -> none  [the longest x1 22.8 us: shards(): totals = lax.psum(partial_errors, 'cond')]
    dynamic_slice x32 -> x0, local copies, waits for them, and re-layouts: 18.7 us -> none  [the longest x20 12.3 us: shards(): partial_errors = lax.map(cond_error, (my_spectra, my_dose))]
    squeeze x14 -> x0, local copies, waits for them, and re-layouts: 13.3 us -> none  [the longest x12 13.3 us: shards(): partial_errors = lax.map(cond_error, (my_spectra, my_dose))]
    reduce_sum x16 -> x0, other arithmetic: 12.8 us -> none  [the longest x8 9.61 us: tile_error(): return jnp.sum(missed * missed)]
    mul x9 -> x0, other arithmetic: 11.8 us -> none  [the longest x8 10.3 us: tile_error(): resist = jax.nn.sigmoid(STEEPNESS * (dose * intensity - THRESHOLD))]
  transfers between devices with their start and end apart: 5 -> 0, of which waited for: 3 -> 0; matrix products, arithmetic and copies ran while one was open for 3% -> 0% of each run, Pallas kernels for 0% -> 0%
where the time goes in v1:
time: 44.7 us; the launch traced here: 44.4 us
  Pallas kernels  34.6 us (77%)
  local copies, waits for them, and re-layouts  9.21 us (21%)
  between operations  0.64 us (1%)
    pallas_call x1, Pallas kernels, shards(): pl.pallas_call(functools.partial(kernel, sizes), out_shape=(jax.ShapeDtyp...  34.6 us
    unnamed x3, local copies, waits for them, and re-layouts  8.01 us
    slice x1, local copies, waits for them, and re-layouts, shards(): return (mask_gradient, loss[0, :1])  1.2 us

profile of v1, /device:TPU:0, one launch (start us, length us, event | category | flops | bytes accessed | tf_op | source)
XLA Modules:
  0.0 44.4 jit_solution(7169551790811287220)
XLA Ops:
  0.6 1.6 %copy.18.latent_ref = f32[256,64]{1,0:T(8,128)} copy(f32[256,64]{0,1:T(8,128)} %param.16) | data formatting | bytes 131072 | tf_op args[0]
  2.2 4.8 %copy.19.table_hbm = f32[8,8,2,65,65]{4,3,2,1,0:T(8,128)} copy(f32[8,8,2,65,65]{4,2,3,1,0:T(2,128)} %param.18) | data formatting | bytes 4326400 | tf_op args[2]
  7.0 34.6 %litho.1 = (f32[256,64]{1,0:T(8,128)}, f32[8,128]{1,0:T(8,128)}) custom-call(f32[256,64]{1,0:T(8,128)} %copy.18.latent_ref, s32[2048,128]{1,0:T(8,128)} %target_hbm.1, f32[8,8,2,65,65]{4,3,2,1,0:T(8,128)} %copy.19.table_hbm, f32[8]{0:T(128)} %socs_ref.1, f32[4]{0:T(128)} %dose_ref.1, s32[8]{0:T(128)} %focus_ref.1, s32[8]{0:T(128)} %level_ref.1, ...), custom_call_target="tpu_custom_call" | custom-call | tf_op jit(solution)/shard_map/litho/pallas_call | solution.py:462
  41.6 1.2 %slice.3 = f32[1,1]{1,0:T(1,128)} slice(f32[8,128]{1,0:T(8,128)} %get-tuple-element.5), slice={[0:1], [0:1]} | slice | bytes 8 | tf_op jit(solution)/shard_map/slice | solution.py:499
  42.8 1.6 %copy.20 = f32[256,64]{0,1:T(8,128)} copy(f32[256,64]{1,0:T(8,128)} %get-tuple-element.6) | data formatting | bytes 131072

commit v2 on v1

--- a/solution.py
+++ b/solution.py
@@ -93,6 +93,10 @@
 def data_right(table, values):
     high, low = split(values)
     return mul(table, jnp.concatenate([high, low, high], axis=0))
+
+
+def flip(index, bit):
+    return index + bit - 2 * bit * ((index // bit) % 2)
 
 
 def kernel(
@@ -128,6 +132,7 @@
     upper,
     lower,
     errors,
+    arrived,
     local_sem,
     mask_send,
     mask_recv,
@@ -141,12 +146,14 @@
     j = lax.axis_index("tile")
     i = lax.axis_index("cond")
     tiles = rows // TILE
-    me = i * parts + j
-    everyone = parts * groups
+    levels = groups.bit_length() - 1
+    assert groups == 1 << levels
     inverse_area = 1.0 / (EXT * EXT)
 
     table_copy = pltpu.make_async_copy(
-        table_hbm.at[pl.ds(j * conds, conds)], raw, local_sem.at[0]
+        table_hbm.at[pl.ds(pl.multiple_of(j * raw.shape[0], 8), raw.shape[0])],
+        raw,
+        local_sem.at[0],
     )
     table_copy.start()
     target_copy = pltpu.make_async_copy(
@@ -154,22 +161,33 @@
     )
     target_copy.start()
 
-    errors[j, i] = jnp.zeros(errors.shape[2:], jnp.float32)
+    errors[0] = jnp.zeros(errors.shape[1:], jnp.float32)
     upper[...] = jnp.zeros_like(upper)
     lower[...] = jnp.zeros_like(lower)
 
     barrier = pltpu.get_barrier_semaphore()
 
-    def greet(step, carry):
-        other = (me + step) % everyone
-        pl.semaphore_signal(
-            barrier, inc=1, device_id=(g, other % parts, other // parts), device_id_type=MESH
-        )
-        return carry
-
-    lax.fori_loop(1, everyone, greet, 0)
-
-    mask_own = jax.nn.sigmoid(latent_ref[...])
+    def greet(core, group):
+        pl.semaphore_signal(barrier, inc=1, device_id=(g, core, group), device_id_type=MESH)
+
+    @pl.when(i > 0)
+    def _():
+        for d in range(parts):
+            greet((j + d) % parts, i - 1)
+
+    @pl.when(i < groups - 1)
+    def _():
+        for d in range(parts):
+            greet((j + d) % parts, i + 1)
+
+    for level in range(1, levels):
+        greet(j, flip(i, 1 << level))
+    for d in range(1, parts):
+        greet((j + d) % parts, i)
+
+    sides = jnp.where(i > 0, 1, 0) + jnp.where(i < groups - 1, 1, 0)
+
+    mask_own = jax.nn.sigmoid(latent_ref[...]).T
     mask[j, HALO : HALO + rows, :] = mask_own
     grad[...] = jnp.zeros_like(grad)
 
@@ -183,7 +201,21 @@
         for h in range(parts):
             mask[h, HALO + rows :, :] = jnp.zeros((HALO, TILE // parts), jnp.float32)
 
-    pl.semaphore_wait(barrier, everyone - 1)
+    table_copy.wait()
+    kern[...] = jnp.zeros_like(kern)
+
+    def pad_kernels(c, carry):
+        for k in range(kernels):
+            for part in range(2):
+                start = (c * kernels + k) * (2 * NF) + part
+                kern[c, k, part, 0:NF, 0:NF] = raw[pl.ds(start, NF, stride=2), :]
+        return carry
+
+    lax.fori_loop(0, conds, pad_kernels, 0)
+
+    target_copy.wait()
+
+    pl.semaphore_wait(barrier, sides * parts + (levels - 1) + (parts - 1))
 
     def mask_peer(d):
         block = mask.at[j, pl.ds(HALO, rows)]
@@ -213,19 +245,6 @@
     def _():
         for d in range(parts):
             mask_edge(False, d).start()
-
-    table_copy.wait()
-    kern[...] = jnp.zeros_like(kern)
-
-    def pad_kernels(c, carry):
-        for k in range(kernels):
-            for part in range(2):
-                kern[c, k, part, 0:NF, 0:NF] = raw[c, k, part]
-        return carry
-
-    lax.fori_loop(0, conds, pad_kernels, 0)
-
-    target_copy.wait()
 
     for d in range(1, parts):
         mask_peer(d).wait()
@@ -297,24 +316,20 @@
         missed = resist - wanted
         slope[index] = (4.0 * STEEPNESS) * dose * (missed * (resist * (1.0 - resist)))
         sums = jnp.sum(missed * missed, axis=0, keepdims=True)
-        errors[j, i, pl.ds(c, 1), :] = errors[j, i, pl.ds(c, 1), :] + sums
+        errors[0, pl.ds(c, 1), :] = errors[0, pl.ds(c, 1), :] + sums
         return carry
 
     lax.fori_loop(0, conds * tiles, forward, 0)
 
-    def err_copy(step):
-        other = (me + step) % everyone
-        block = errors.at[j, i]
+    def err_copy(n):
+        if n < levels:
+            device, slot = (g, j, flip(i, 1 << n)), n
+        else:
+            device, slot = (g, (j + n - levels + 1) % parts, i), levels
         return pltpu.make_async_remote_copy(
-            block, block, err_send.at[step], err_recv.at[step],
-            device_id=(g, other % parts, other // parts), device_id_type=MESH,
+            errors.at[slot], arrived.at[n], err_send.at[n], err_recv.at[n],
+            device_id=device, device_id_type=MESH,
         )
-
-    def send_error(step, carry):
-        err_copy(step).start()
-        return carry
-
-    lax.fori_loop(1, everyone, send_error, 0)
 
     def backward(index, carry):
         c = index // tiles
@@ -348,28 +363,30 @@
         dspec[index, FP:, :] = imag
         return carry
 
-    lax.fori_loop(0, conds * tiles, backward, 0)
-
-    def wait_error(step, carry):
-        err_copy(step).wait()
-        return carry
-
-    lax.fori_loop(1, everyone, wait_error, 0)
-
-    slots = errors.shape[2]
+    steps = conds * tiles
+    rounds = levels + 1
+    for n in range(rounds):
+        copies = [err_copy(n)] if n < levels else [err_copy(levels + d) for d in range(parts - 1)]
+        for copy in copies:
+            copy.start()
+        lax.fori_loop(n * steps // rounds, (n + 1) * steps // rounds, backward, 0)
+        for copy in copies:
+            copy.wait()
+        if n < levels:
+            errors[n + 1] = errors[n] + arrived[n]
+
+    slots = errors.shape[1]
     valid = lax.broadcasted_iota(jnp.int32, (slots, 1), 0) < conds
-    denominator = jnp.zeros((1, 1), jnp.float32)
-    mine = jnp.zeros((slots, 1), jnp.float32)
-    for h in range(parts):
-        total = errors[h, 0]
-        for n in range(1, groups):
-            total = total + errors[h, n]
+
+    def exponents(total):
         score = SHARPNESS * jnp.sum(total, axis=1, keepdims=True) / pixels
-        exponent = jnp.where(valid, jnp.exp(score), 0.0)
-        denominator = denominator + jnp.sum(exponent, axis=0, keepdims=True)
-        mine = jnp.where(j == h, exponent, mine)
+        return jnp.where(valid, jnp.exp(score), 0.0)
+
+    mine = exponents(errors[levels])
+    sums = [mine] + [exponents(arrived[levels + d]) for d in range(parts - 1)]
+    denominator = functools.reduce(jnp.add, [jnp.sum(e, axis=0, keepdims=True) for e in sums])
     weights = mine / denominator
-    loss_out[...] = jnp.broadcast_to(jnp.log(denominator) / SHARPNESS, loss_out.shape)
+    loss_out[...] = jnp.log(denominator) / SHARPNESS
 
     for t in range(tiles):
         total = jnp.zeros((2 * FP, GP), jnp.float32)
@@ -437,9 +454,10 @@
     for d in range(1, parts):
         head = head + upper[d]
         tail = tail + lower[d]
-    grad_out[...] = total * scale
-    grad_out[0:HALO, :] = (total[0:HALO] + head) * scale[0:HALO]
-    grad_out[rows - HALO :, :] = (total[rows - HALO :] + tail) * scale[rows - HALO :]
+    total = jnp.concatenate(
+        [total[:HALO] + head, total[HALO : rows - HALO], total[rows - HALO :] + tail], axis=0
+    )
+    grad_out[...] = (total * scale).T
 
 
 def shards(latent, target, kernel_table, socs_weights, dose_levels, cond_focus, cond_dose):
@@ -451,6 +469,7 @@
     conds = all_conds // parts
     tiles = rows // TILE
     pixels = rows * groups * TILE
+    spectra = kernel_table.transpose(0, 1, 3, 2, 4).reshape(-1, NF)
     tables = [jnp.asarray(table) for table in make_tables(parts)]
     sizes = (parts, groups, rows, conds, kernels, pixels, all_conds, dose_levels.shape[0])
     slots = -(-conds // 8) * 8
@@ -458,18 +477,18 @@
     smem = pl.BlockSpec(memory_space=pltpu.SMEM)
     anywhere = pl.BlockSpec(memory_space=pl.ANY)
     f32 = jnp.float32
-    everyone = parts * groups
+    levels = groups.bit_length() - 1
     mask_gradient, loss = pl.pallas_call(
         functools.partial(kernel, sizes),
         out_shape=(
-            jax.ShapeDtypeStruct((rows, width), f32),
-            jax.ShapeDtypeStruct((8, 128), f32),
+            jax.ShapeDtypeStruct((width, rows), f32),
+            jax.ShapeDtypeStruct((1, 1), f32),
         ),
         in_specs=[vmem, anywhere, anywhere, smem, smem, smem, smem] + [vmem] * len(tables),
         out_specs=(vmem, vmem),
         scratch_shapes=[
             pltpu.VMEM((parts, rows + 2 * HALO, width), f32),
-            pltpu.VMEM((conds,) + kernel_table.shape[1:], f32),
+            pltpu.VMEM((conds * kernels * 2 * NF, NF), f32),
             pltpu.VMEM((conds, kernels, 2, FP, GP), f32),
             pltpu.VMEM((rows, TILE), jnp.int32),
             pltpu.VMEM((tiles, 2 * FP, GP), f32),
@@ -480,12 +499,13 @@
             pltpu.VMEM((max(parts - 1, 1), rows, width), f32),
             pltpu.VMEM((parts, HALO, width), f32),
             pltpu.VMEM((parts, HALO, width), f32),
-            pltpu.VMEM((parts, groups, slots, TILE), f32),
+            pltpu.VMEM((levels + 1, slots, TILE), f32),
+            pltpu.VMEM((levels + parts - 1, slots, TILE), f32),
             pltpu.SemaphoreType.DMA((2,)),
             pltpu.SemaphoreType.DMA((3 * parts,)),
             pltpu.SemaphoreType.DMA((3 * parts,)),
-            pltpu.SemaphoreType.DMA((everyone,)),
-            pltpu.SemaphoreType.DMA((everyone,)),
+            pltpu.SemaphoreType.DMA((levels + parts - 1,)),
+            pltpu.SemaphoreType.DMA((levels + parts - 1,)),
             pltpu.SemaphoreType.DMA((3 * parts,)),
             pltpu.SemaphoreType.DMA((3 * parts,)),
         ],
@@ -494,9 +514,9 @@
         ),
         name="litho",
     )(
-        latent, target, kernel_table, socs_weights, dose_levels, cond_focus, cond_dose, *tables
+        latent.T, target, spectra, socs_weights, dose_levels, cond_focus, cond_dose, *tables
     )
-    return (mask_gradient, loss[0, :1])
+    return (mask_gradient.T, loss.reshape(1))
 
 
 def solution(mesh):

time: 44.7 us -> 38.3 us (0.86)
  local copies, waits for them, and re-layouts: 9.21 us -> 1.47 us
  between operations: 0.64 us -> 2.39 us
    unnamed x3 -> x1, local copies, waits for them, and re-layouts: 8.01 us -> 1.47 us
    slice x1 -> x0, local copies, waits for them, and re-layouts: 1.2 us -> none  [shards(): return (mask_gradient, loss[0, :1])]
where the time goes in v2:
time: 38.3 us; the launch traced here: 38.1 us
  Pallas kernels  34.2 us (89%)
  between operations  2.39 us (6%)
  local copies, waits for them, and re-layouts  1.47 us (4%)
    pallas_call x1, Pallas kernels, shards(): pl.pallas_call(functools.partial(kernel, sizes), out_shape=(jax.ShapeDtyp...  34.2 us
    unnamed x1, local copies, waits for them, and re-layouts  1.47 us

profile of v2, /device:TPU:0, one launch (start us, length us, event | category | flops | bytes accessed | tf_op | source)
XLA Modules:
  0.0 38.1 jit_solution(11482159685969620703)
XLA Ops:
  0.6 34.2 %litho.1 = (f32[64,256]{1,0:T(8,128)}, f32[1,1]{1,0:T(1,128)}) custom-call(f32[64,256]{1,0:T(8,128)} %bitcast.7, s32[2048,128]{1,0:T(8,128)} %target_hbm.1, f32[8320,65]{1,0:T(8,128)} %bitcast.6, f32[8]{0:T(128)} %socs_ref.1, f32[4]{0:T(128)} %dose_ref.1, s32[8]{0:T(128)} %focus_ref.1, s32[8]{0:T(128)} %level_ref.1, ...), custom_call_target="tpu_custom_call" | custom-call | tf_op jit(solution)/shard_map/litho/pallas_call | solution.py:481
  34.8 1.5 %copy.20 = f32[256,64]{0,1:T(8,128)} copy(f32[256,64]{0,1:T(8,128)} %bitcast.8) | data formatting | bytes 131072

commit v3 on v2

--- a/solution.py
+++ b/solution.py
@@ -108,6 +108,17 @@
     dose_ref,
     focus_ref,
     level_ref,
+    col_high_hbm,
+    col_low_hbm,
+    col_back_hbm,
+    spec_tab_hbm,
+    spec_back_hbm,
+    row_tab_hbm,
+    row_back_hbm,
+    field_tab_hbm,
+    field_back_hbm,
+    grad_out,
+    loss_out,
     col_high,
     col_low,
     col_back,
@@ -117,8 +128,6 @@
     row_back,
     field_tab,
     field_back,
-    grad_out,
-    loss_out,
     mask,
     raw,
     kern,
@@ -134,6 +143,7 @@
     errors,
     arrived,
     local_sem,
+    wave_sem,
     mask_send,
     mask_recv,
     err_send,
@@ -161,6 +171,23 @@
     )
     target_copy.start()
 
+    waves = (
+        (col_high_hbm, col_high),
+        (col_low_hbm, col_low),
+        (spec_tab_hbm, spec_tab),
+        (row_tab_hbm, row_tab),
+        (field_tab_hbm, field_tab),
+        (field_back_hbm, field_back),
+        (row_back_hbm, row_back),
+        (spec_back_hbm, spec_back),
+        (col_back_hbm, col_back),
+    )
+    wave_copies = [
+        pltpu.make_async_copy(src, dst, wave_sem.at[n]) for n, (src, dst) in enumerate(waves)
+    ]
+    for copy in wave_copies:
+        copy.start()
+
     errors[0] = jnp.zeros(errors.shape[1:], jnp.float32)
     upper[...] = jnp.zeros_like(upper)
     lower[...] = jnp.zeros_like(lower)
@@ -214,6 +241,8 @@
     lax.fori_loop(0, conds, pad_kernels, 0)
 
     target_copy.wait()
+    for copy in wave_copies:
+        copy.wait()
 
     pl.semaphore_wait(barrier, sides * parts + (levels - 1) + (parts - 1))
 
@@ -319,7 +348,7 @@
         errors[0, pl.ds(c, 1), :] = errors[0, pl.ds(c, 1), :] + sums
         return carry
 
-    lax.fori_loop(0, conds * tiles, forward, 0)
+    lax.fori_loop(0, conds * tiles, forward, 0, unroll=2)
 
     def err_copy(n):
         if n < levels:
@@ -369,7 +398,7 @@
         copies = [err_copy(n)] if n < levels else [err_copy(levels + d) for d in range(parts - 1)]
         for copy in copies:
             copy.start()
-        lax.fori_loop(n * steps // rounds, (n + 1) * steps // rounds, backward, 0)
+        lax.fori_loop(n * steps // rounds, (n + 1) * steps // rounds, backward, 0, unroll=2)
         for copy in copies:
             copy.wait()
         if n < levels:
@@ -484,9 +513,10 @@
             jax.ShapeDtypeStruct((width, rows), f32),
             jax.ShapeDtypeStruct((1, 1), f32),
         ),
-        in_specs=[vmem, anywhere, anywhere, smem, smem, smem, smem] + [vmem] * len(tables),
+        in_specs=[vmem, anywhere, anywhere, smem, smem, smem, smem] + [anywhere] * len(tables),
         out_specs=(vmem, vmem),
-        scratch_shapes=[
+        scratch_shapes=[pltpu.VMEM(table.shape, table.dtype) for table in tables]
+        + [
             pltpu.VMEM((parts, rows + 2 * HALO, width), f32),
             pltpu.VMEM((conds * kernels * 2 * NF, NF), f32),
             pltpu.VMEM((conds, kernels, 2, FP, GP), f32),
@@ -502,6 +532,7 @@
             pltpu.VMEM((levels + 1, slots, TILE), f32),
             pltpu.VMEM((levels + parts - 1, slots, TILE), f32),
             pltpu.SemaphoreType.DMA((2,)),
+            pltpu.SemaphoreType.DMA((len(tables),)),
             pltpu.SemaphoreType.DMA((3 * parts,)),
             pltpu.SemaphoreType.DMA((3 * parts,)),
             pltpu.SemaphoreType.DMA((levels + parts - 1,)),

time: 38.3 us -> 37.3 us (0.974)
  Pallas kernels: 34.2 us -> 33.2 us
    pallas_call x1, Pallas kernels: 34.2 us -> 33.2 us  [shards(): pl.pallas_call(functools.partial(kernel, sizes), out_shape=(jax.ShapeDtyp...]
where the time goes in v3:
time: 37.3 us; the launch traced here: 37.1 us
  Pallas kernels  33.2 us (89%)
  between operations  2.39 us (6%)
  local copies, waits for them, and re-layouts  1.47 us (4%)
    pallas_call x1, Pallas kernels, shards(): pl.pallas_call(functools.partial(kernel, sizes), out_shape=(jax.ShapeDtyp...  33.2 us
    unnamed x1, local copies, waits for them, and re-layouts  1.47 us

profile of v3, /device:TPU:0, one launch (start us, length us, event | category | flops | bytes accessed | tf_op | source)
XLA Modules:
  0.0 37.1 jit_solution(9360081501617074783)
XLA Ops:
  0.6 33.2 %litho.1 = (f32[64,256]{1,0:T(8,128)}, f32[1,1]{1,0:T(1,128)}) custom-call(f32[64,256]{1,0:T(8,128)} %bitcast.7, s32[2048,128]{1,0:T(8,128)} %target_hbm.1, f32[8320,65]{1,0:T(8,128)} %bitcast.6, f32[8]{0:T(128)} %socs_ref.1, f32[4]{0:T(128)} %dose_ref.1, s32[8]{0:T(128)} %focus_ref.1, s32[8]{0:T(128)} %level_ref.1, ...), custom_call_target="tpu_custom_call" | custom-call | tf_op jit(solution)/shard_map/litho/pallas_call | solution.py:510
  33.8 1.5 %copy.20 = f32[256,64]{0,1:T(8,128)} copy(f32[256,64]{0,1:T(8,128)} %bitcast.8) | data formatting | bytes 131072
